TPU v7x, 32 devices: a whole 2x2x4 slice. The times are simulated.
32 devices in a mesh: grp: 4 (over y, x), dev: 8 (over z, core).
Axes of the slice: x: 2, y: 2, z: 4, core: 2. Of those that a mesh axis runs over, the one named last changes fastest.
Arguments:
- embeddings: bfloat16 [32768, 1024], P(('grp', 'dev')), may hold values from -6 to 6
- cluster_ids: int32 [32768, 1], P(('grp', 'dev')), may hold values from 0 to 255; in each aligned block of 1024 rows (0 to 1023, 1024 to 2047, ...) at most 8 rows name the same one
- cluster_slot: int32 [256], replicated, may hold values from 0 to 255, each once
Outputs:
- max_cosine: float32 [32768], P(('grp', 'dev'))
- centroids: float32 [256, 1024], P(('grp', 'dev'))
All inputs are finite; a program needn't handle non-finite values.
Results may differ from a plain program's by a relative error of at most 0.0029.
Values may be sent and summed in bfloat16 or wider, within the bound.
A program may use at most 128 MiB of HBM per device.

v0:
```python
import jax
import jax.numpy as jnp
from jax import lax
from jax.sharding import PartitionSpec as P

MOST = 8


def local(embeddings, cluster_ids, cluster_slot):
    n_grp = lax.axis_size("grp")
    n_dev = lax.axis_size("dev")
    ndev = n_grp * n_dev
    rows_dev = embeddings.shape[0]
    width = embeddings.shape[1]
    clusters = cluster_slot.shape[0]
    owned = clusters // ndev
    emb32 = embeddings.astype(jnp.float32)
    normalized = (emb32 * lax.rsqrt(jnp.sum(emb32 * emb32, axis=1, keepdims=True) + 1e-06)).astype(
        jnp.bfloat16
    )
    ids = cluster_ids[:, 0]
    order = jnp.arange(rows_dev, dtype=jnp.int32)
    same = (ids[:, None] == ids[None, :]) & (order[None, :] < order[:, None])
    ranks = jnp.sum(same.astype(jnp.int32), axis=1)
    labels = jnp.arange(clusters, dtype=jnp.int32)
    slots = jnp.sum(jnp.where(ids[:, None] == labels[None, :], cluster_slot[None, :], 0), axis=1)
    place = slots * MOST + ranks
    outgoing = jnp.zeros((clusters * MOST, width), jnp.bfloat16).at[place].set(normalized)
    received = lax.all_to_all(
        outgoing.reshape(ndev, owned, MOST, width),
        ("grp", "dev"),
        split_axis=0,
        concat_axis=0,
        tiled=True,
    )
    live = jnp.sum(jnp.square(received.astype(jnp.float32)), axis=3) > 0.5
    gram = jnp.einsum("sckd,tcld->csktl", received, received, preferred_element_type=jnp.float32)
    source_eq = jnp.arange(ndev)[:, None, None, None] == jnp.arange(ndev)[None, None, :, None]
    rank_eq = jnp.arange(MOST)[None, :, None, None] == jnp.arange(MOST)[None, None, None, :]
    selfpair = source_eq & rank_eq
    keep = jnp.transpose(live, (1, 0, 2))[:, None, None, :, :] & ~selfpair[None]
    maxima = jnp.max(jnp.where(keep, gram, -1.0), axis=(3, 4))
    returned = lax.all_to_all(
        jnp.transpose(maxima, (1, 0, 2)), ("grp", "dev"), split_axis=0, concat_axis=0, tiled=True
    )
    max_cosine = returned.reshape(-1)[place]
    columns = jnp.arange(owned * lax.axis_size(("grp", "dev")), dtype=jnp.int32)
    onehot = (slots[:, None] == columns[None, :]).astype(jnp.bfloat16)
    sums = lax.psum_scatter(
        lax.dot_general(
            onehot, normalized, (((0,), (0,)), ((), ())), preferred_element_type=jnp.float32
        ),
        ("grp", "dev"),
        scatter_dimension=0,
        tiled=True,
    )
    centroids = sums * lax.rsqrt(jnp.sum(sums * sums, axis=1, keepdims=True) + 1e-06)
    return (max_cosine, centroids)


def solution(mesh):
    in_specs = (P(("grp", "dev"), None), P(("grp", "dev"), None), P())
    out_specs = (P(("grp", "dev")), P(("grp", "dev"), None))
    return jax.shard_map(local, mesh=mesh, in_specs=in_specs, out_specs=out_specs, check_vma=False)
```

profile of v0, /device:TPU:0, one launch (start us, length us, event | category | flops | bytes accessed | tf_op | source)
XLA Modules:
  0.0 216.8 jit_solution(18030413643251129048)
XLA Ops:
  7.2 1.3 convert_reduce_fusion
  8.4 1.1 select_reduce_fusion.1
  9.5 2.1 fusion
  11.6 8.9 %scatter_custom_fusion = bf16[2048,1024]{1,0:T(8,128)(2,1)} fusion(s32[1024]{0:T(1024)S(1)} %bitcast.12, bf16[]{:T(256)} %constant.9.clone.1, bf16[1024,1024]{1,0:T(8,128)(2,1)} %param.3, f32[1024]{0:T(1024)S(1)} %add_rsqrt_fusion), kind=kCustom, calls=%fused_computation.14 | custom fusion | flops 3145728 | bytes 6295554 | tf_op jit(solution)/shard_map/scatter | solution.py:28
  20.5 0.0 copy-start
  20.5 7.4 %all-to-all-start = ((bf16[32,8,8,1024]{3,2,1,0:T(8,128)(2,1)}), bf16[32,8,8,1024]{3,2,1,0:T(8,128)(2,1)}, u32[]{:S(2)}, u32[]{:S(2)}) async-start(bf16[32,8,8,1024]{3,2,1,0:T(8,128)(2,1)} %bitcast.9), calls=%async_computation | async-start | bytes 8388608 | tf_op jit(solution)/shard_map/all_to_all | solution.py:29
  27.9 0.2 reduce-scatter.2.cloned.1.call-start
  28.2 0.0 copy-done
  28.2 2.1 fusion.12
  30.3 0.0 reduce-scatter.2.cloned.1.call-update
  30.3 0.2 and_not_fusion
  30.6 141.3 %reduce-scatter.2.cloned.1.call-done = f32[8,1024]{1,0:T(8,128)} async-done(((f32[256,1024]{1,0:T(8,128)}), f32[8,1024]{1,0:T(8,128)}) %reduce-scatter.2.cloned.1.call-update) | async-done | bytes 32784 | tf_op jit(solution)/shard_map/reduce_scatter | solution.py:49
  171.8 0.9 multiply_reduce_fusion.1
  172.7 0.0 all-to-all-done
  172.7 3.1 %multiply_reduce_fusion = f32[32,8,8]{2,1,0:T(8,128)S(1)} fusion(bf16[32,8,8,1024]{3,2,1,0:T(8,128)(2,1)} %all-to-all-done), kind=kLoop, calls=%fused_computation.3 | loop fusion | flops 6289408 | bytes 4202496 | tf_op jit(solution)/shard_map/reduce_sum | solution.py:36
  175.8 0.1 copy.15
  176.0 0.0 copy-start.1
  176.0 11.9 %select_reduce_fusion = f32[8,32,8]{2,1,0:T(8,128)S(1)} fusion(pred[32,8,32,8]{2,1,3,0:T(8,128)(4,1)S(1)} %and_not_fusion, pred[8,32,8]{1,2,0:T(8,128)(4,1)S(1)} %copy.15, bf16[32,8,8,1024,1]{3,2,1,0,4:T(8,128)(2,1)} %bitcast.5), kind=kOutput, calls=%fused_computation.2 | convolution fusion | flops 1075312640 | bytes 4270080 | tf_op jit(solution)/shard_map/sckd,tcld->csktl/dot_general | solution.py:37
  187.9 0.7 copy.18
  188.6 2.6 %all-to-all-start.1 = ((f32[32,8,8]{2,1,0:T(8,128)}), f32[32,8,8]{2,1,0:T(8,128)S(1)}, u32[]{:S(2)}, u32[]{:S(2)}) async-start(f32[32,8,8]{2,1,0:T(8,128)} %copy.18), calls=%async_computation.1 | async-start | bytes 262144 | tf_op jit(solution)/shard_map/all_to_all | solution.py:43
  191.2 0.0 copy-done.1
  191.2 0.7 broadcast_multiply_fusion
  191.9 7.5 %all-to-all-done.1 = f32[32,8,8]{2,1,0:T(8,128)S(1)} async-done(((f32[32,8,8]{2,1,0:T(8,128)}), f32[32,8,8]{2,1,0:T(8,128)S(1)}, u32[]{:S(2)}, u32[]{:S(2)}) %all-to-all-start.1) | async-done | bytes 8224 | tf_op jit(solution)/shard_map/all_to_all | solution.py:43
  199.3 0.1 reshape.86
  199.4 10.5 %gather_fusion = f32[1024]{0:T(1024)} fusion(f32[2048]{0:T(1024)S(1)} %reshape.86, s32[1024]{0:T(1024)S(1)} %broadcast_clamp_fusion), kind=kCustom, calls=%fused_computation | custom fusion | bytes 12288 | tf_op jit(solution)/shard_map/gather | solution.py:46
  (8 shorter events, 0.1 us)
Async XLA Ops:
  20.5 7.7 %copy-start = (bf16[1024,1024]{1,0:T(8,128)(2,1)S(1)}, bf16[1024,1024]{1,0:T(8,128)(2,1)}, u32[]{:S(2)}) copy-start(bf16[1024,1024]{1,0:T(8,128)(2,1)} %param.3) | copy-start | bytes 6291460
  20.5 152.2 %all-to-all-start = ((bf16[32,8,8,1024]{3,2,1,0:T(8,128)(2,1)}), bf16[32,8,8,1024]{3,2,1,0:T(8,128)(2,1)}, u32[]{:S(2)}, u32[]{:S(2)}) async-start(bf16[32,8,8,1024]{3,2,1,0:T(8,128)(2,1)} %bitcast.9), calls=%async_computation | async-start | bytes 8388608 | tf_op jit(solution)/shard_map/all_to_all | solution.py:29
  27.9 143.9 %reduce-scatter.2.cloned.1.call-start = ((), (), s32[]{:S(2)}) async-start(), calls=%async_computation.3 | async-start | bytes 1081344 | tf_op jit(solution)/shard_map/reduce_scatter | solution.py:49
  176.0 15.2 %copy-start.1 = (f32[8,1024]{1,0:T(8,128)S(1)}, f32[8,1024]{1,0:T(8,128)}, u32[]{:S(2)}) copy-start(f32[8,1024]{1,0:T(8,128)} %reduce-scatter.2.cloned.1.call-done) | copy-start | bytes 98308
  188.6 10.7 %all-to-all-start.1 = ((f32[32,8,8]{2,1,0:T(8,128)}), f32[32,8,8]{2,1,0:T(8,128)S(1)}, u32[]{:S(2)}, u32[]{:S(2)}) async-start(f32[32,8,8]{2,1,0:T(8,128)} %copy.18), calls=%async_computation.1 | async-start | bytes 262144 | tf_op jit(solution)/shard_map/all_to_all | solution.py:43
Sparse Core Ops, SparseCore 0:
  31.0 140.7 reduce-scatter.1
where the time goes:
time: 217 us
  waiting for transfers between devices  149 us (69%)
  other arithmetic  18.2 us (8%)
  between operations  14.1 us (6%)
  matrix products  14 us (6%)
  local copies, waits for them, and re-layouts  11.5 us (5%)
  starting transfers between devices  10.2 us (5%)
    reduce_scatter x1, waiting for transfers between devices, local(): lax.psum_scatter(lax.dot_general(onehot, normalized, (((0,), (0,)), ((),...  141 us
    dot_general x1, matrix products, local(): jnp.einsum('sckd,tcld->csktl', received, received, preferred_element_type...  11.9 us
    gather x1, local copies, waits for them, and re-layouts, local(): max_cosine = returned.reshape(-1)[place]  10.5 us
    scatter x1, other arithmetic, local(): jnp.zeros((clusters * MOST, width), jnp.bfloat16).at[place].set(normalized)  8.87 us
    all_to_all x1, waiting for transfers between devices, local(): lax.all_to_all(jnp.transpose(maxima, (1, 0, 2)), ('grp', 'dev'), split_ax...  7.48 us
    all_to_all x1, starting transfers between devices, local(): lax.all_to_all(outgoing.reshape(ndev, owned, MOST, width), ('grp', 'dev')...  7.43 us
  transfers between devices with their start and end apart: 3, of which 2 were waited for; matrix products, arithmetic and copies ran while one was open for 2% of the time, Pallas kernels for 0%

commit v1 on v0

v1 whole, which is shorter than its diff:
```python
import functools

import jax
import jax.numpy as jnp
from jax import lax
from jax.experimental import pallas as pl
from jax.experimental.pallas import tpu as pltpu
from jax.sharding import PartitionSpec as P

MOST = 8
MESH = pl.DeviceIdType.MESH
F32 = jnp.float32
BF16 = jnp.bfloat16
CHUNK = 256


def iota(shape, dim):
    return lax.broadcasted_iota(jnp.int32, shape, dim)


def kernel(
    n_grp,
    n_dev,
    owned,
    quota,
    group,
    emb,
    ids,
    slot_row,
    best_out,
    cent_out,
    norm,
    send,
    recv,
    where_row,
    lab_mat,
    lab_send,
    lab_recv,
    lab_rows,
    lab_cols,
    best,
    ret_send,
    ret_recv,
    ret_mat,
    sums,
    load_sem,
    send_sem,
    recv_sem,
    small_send,
    small_recv,
):
    n = n_grp * n_dev
    rows = norm.shape[0]
    clusters = slot_row.shape[1]
    span = group * quota
    n_groups = n // group
    my_g = lax.axis_index("grp")
    my_d = lax.axis_index("dev")

    def ahead(k):
        return (my_g + k // n_dev) % n_grp, (my_d + k % n_dev) % n_dev

    def behind(k):
        return (my_g + n_grp - k // n_dev) % n_grp, (my_d + n_dev - k % n_dev) % n_dev

    barrier = pltpu.get_barrier_semaphore()

    @pl.loop(1, n)
    def _(k):
        pl.semaphore_signal(barrier, inc=1, device_id=ahead(k), device_id_type=MESH)

    def load(c):
        part = pl.ds(pl.multiple_of(c * CHUNK, CHUNK), CHUNK)
        return pltpu.make_async_copy(emb.at[part], norm.at[part], load_sem.at[c])

    @pl.loop(0, rows // CHUNK)
    def _(c):
        load(c).start()

    eye = iota((clusters, clusters), 0) == iota((clusters, clusters), 1)
    slot_col = jnp.sum(jnp.where(eye, slot_row[...].astype(F32), 0.0), axis=1, keepdims=True)

    lab_mat[...] = jnp.zeros_like(lab_mat)
    before = (iota((CHUNK, CHUNK), 0) < iota((CHUNK, CHUNK), 1)).astype(BF16)
    grp_f = my_g.astype(F32)
    dev_f = my_d.astype(F32)

    def place(c, carry):
        part = pl.ds(pl.multiple_of(c * CHUNK, CHUNK), CHUNK)
        hit = iota((clusters, CHUNK), 0) == ids[:, part]
        slot = jnp.sum(jnp.where(hit, slot_col, 0.0), axis=0, keepdims=True)
        owner = jnp.floor((slot + 0.5) * (1.0 / owned))
        local = slot - owner * owned
        og = jnp.floor((owner + 0.5) * (1.0 / n_dev))
        kg = og - grp_f
        kd = owner - og * n_dev - dev_f
        kg = jnp.where(kg < 0, kg + n_grp, kg)
        kd = jnp.where(kd < 0, kd + n_dev, kd)
        k = kg * n_dev + kd
        mine = iota((n, CHUNK), 0).astype(F32) == k
        hot = mine.astype(F32)
        earlier = jnp.dot(hot.astype(BF16), before, preferred_element_type=F32) + carry
        pos = jnp.sum(hot * earlier, axis=0, keepdims=True)
        gk = jnp.floor((k + 0.5) * (1.0 / group))
        lane = (k - gk * group) * quota + pos
        where_row[0:1, part] = k
        where_row[1:2, part] = lane
        where_row[2:3, part] = k * quota + pos
        spot = (iota((span, CHUNK), 0).astype(F32) == lane).astype(BF16)
        lab_mat[...] += lax.dot_general(
            (hot * (local + 1.0)).astype(BF16),
            spot,
            (((1,), (1,)), ((), ())),
            preferred_element_type=F32,
        )
        return carry + jnp.sum(hot, axis=1, keepdims=True)

    lax.fori_loop(0, rows // CHUNK, place, jnp.zeros((n, 1), F32))

    pl.semaphore_wait(barrier, n - 1)

    lab_recv[0] = lab_mat[0:1, :]

    @pl.loop(1, n)
    def _(k):
        lab_send[k] = lab_mat[pl.ds(k, 1), :]
        pltpu.make_async_remote_copy(
            src_ref=lab_send.at[k],
            dst_ref=lab_recv.at[k],
            send_sem=small_send.at[0],
            recv_sem=small_recv.at[0],
            device_id=ahead(k),
            device_id_type=MESH,
        ).start()

    @pl.loop(0, rows // CHUNK)
    def _(c):
        load(c).wait()
        part = pl.ds(pl.multiple_of(c * CHUNK, CHUNK), CHUNK)
        x = norm[part, :].astype(F32)
        norm[part, :] = (x * lax.rsqrt(jnp.sum(x * x, axis=1, keepdims=True) + 1e-06)).astype(BF16)

    @pl.loop(0, n_groups)
    def _(g):
        spots = (iota((span, rows), 0) + g * span).astype(F32) == where_row[2:3, :]
        block = jnp.dot(spots.astype(BF16), norm[...], preferred_element_type=F32).astype(BF16)
        send[pl.ds(pl.multiple_of(g * span, span), span), :] = block

        @pl.when(g == 0)
        def _():
            recv[0:quota, :] = block[0:quota]

        @pl.loop(0, group)
        def _(j):
            k = g * group + j

            @pl.when(k > 0)
            def _():
                part = pl.ds(pl.multiple_of(k * quota, quota), quota)
                pltpu.make_async_remote_copy(
                    src_ref=send.at[part],
                    dst_ref=recv.at[part],
                    send_sem=send_sem,
                    recv_sem=recv_sem.at[g],
                    device_id=ahead(k),
                    device_id_type=MESH,
                ).start()

    others = lab_recv.at[pl.ds(1, n - 1)]
    pltpu.make_async_copy(others, others, small_recv.at[0]).wait()
    diag = iota((span, span), 0) == iota((span, span), 1)

    @pl.loop(0, n_groups)
    def _(g):
        row = lab_recv[g * group]
        for j in range(1, group):
            row = row + lab_recv[g * group + j]
        lab_rows[g] = row
        lab_cols[g] = jnp.sum(jnp.where(diag, row, 0.0), axis=1, keepdims=True)
        best[g] = jnp.full((1, span), -1.0, F32)

    sums[...] = jnp.zeros_like(sums)

    def contract(a, b):
        return lax.dot_general(a, b, (((1,), (1,)), ((), ())), preferred_element_type=F32)

    @pl.loop(0, n_groups)
    def _(g):
        @pl.when(g == 0)
        def _():
            got = recv.at[pl.ds(quota, span - quota)]
            pltpu.make_async_copy(got, got, recv_sem.at[0]).wait()

        @pl.when(g > 0)
        def _():
            got = recv.at[pl.ds(pl.multiple_of(g * span, span), span)]
            pltpu.make_async_copy(got, got, recv_sem.at[g]).wait()

        new = recv[pl.ds(pl.multiple_of(g * span, span), span), :]
        member = iota((owned, span), 0).astype(F32) + 1.0 == lab_rows[g]
        sums[...] += jnp.dot(member.astype(BF16), new, preferred_element_type=F32)

        keep = (lab_cols[g] == lab_rows[g]) & ~diag
        top = jnp.max(jnp.where(keep, contract(new, new), -1.0), axis=0, keepdims=True)
        best[g] = jnp.maximum(best[g], top)

        @pl.loop(0, g)
        def _(h):
            old = recv[pl.ds(pl.multiple_of(h * span, span), span), :]
            keep = lab_cols[h] == lab_rows[g]
            top = jnp.max(jnp.where(keep, contract(old, new), -1.0), axis=0, keepdims=True)
            best[g] = jnp.maximum(best[g], top)
            keep = lab_cols[g] == lab_rows[h]
            top = jnp.max(jnp.where(keep, contract(new, old), -1.0), axis=0, keepdims=True)
            best[h] = jnp.maximum(best[h], top)

    ret_recv[0] = best[0]

    @pl.loop(1, n)
    def _(k):
        ret_send[k] = best[k // group]
        pltpu.make_async_remote_copy(
            src_ref=ret_send.at[k],
            dst_ref=ret_recv.at[k],
            send_sem=small_send.at[1],
            recv_sem=small_recv.at[1],
            device_id=behind(k),
            device_id_type=MESH,
        ).start()

    total = sums[...]
    cent_out[...] = total * lax.rsqrt(jnp.sum(total * total, axis=1, keepdims=True) + 1e-06)

    back = ret_recv.at[pl.ds(1, n - 1)]
    pltpu.make_async_copy(back, back, small_recv.at[1]).wait()

    @pl.loop(0, n)
    def _(k):
        ret_mat[pl.ds(k, 1), :] = ret_recv[k]

    @pl.loop(0, rows // CHUNK)
    def _(c):
        part = pl.ds(pl.multiple_of(c * CHUNK, CHUNK), CHUNK)
        hot = (iota((n, CHUNK), 0).astype(F32) == where_row[0:1, part]).astype(F32)
        picked = lax.dot_general(
            ret_mat[...],
            hot,
            (((0,), (0,)), ((), ())),
            precision=lax.Precision.HIGHEST,
            preferred_element_type=F32,
        )
        spot = iota((span, CHUNK), 0).astype(F32) == where_row[1:2, part]
        best_out[:, part] = jnp.sum(jnp.where(spot, picked, 0.0), axis=0, keepdims=True)

    sent = send.at[pl.ds(quota, n * quota - quota)]
    pltpu.make_async_copy(sent, sent, send_sem).wait()
    sent = lab_send.at[pl.ds(1, n - 1)]
    pltpu.make_async_copy(sent, sent, small_send.at[0]).wait()
    sent = ret_send.at[pl.ds(1, n - 1)]
    pltpu.make_async_copy(sent, sent, small_send.at[1]).wait()


def local(embeddings, cluster_ids, cluster_slot):
    n_grp = lax.axis_size("grp")
    n_dev = lax.axis_size("dev")
    n = n_grp * n_dev
    rows, width = embeddings.shape
    clusters = cluster_slot.shape[0]
    owned = clusters // n
    quota = owned * MOST
    group = 4
    span = group * quota
    groups = n // group
    vmem = pl.BlockSpec(memory_space=pltpu.VMEM)
    best, cent = pl.pallas_call(
        functools.partial(kernel, n_grp, n_dev, owned, quota, group),
        out_shape=(
            jax.ShapeDtypeStruct((1, rows), F32),
            jax.ShapeDtypeStruct((owned, width), F32),
        ),
        in_specs=[pl.BlockSpec(memory_space=pl.ANY), vmem, vmem],
        out_specs=(vmem, vmem),
        scratch_shapes=[
            pltpu.VMEM((rows, width), BF16),
            pltpu.VMEM((n * quota, width), BF16),
            pltpu.VMEM((n * quota, width), BF16),
            pltpu.VMEM((8, rows), F32),
            pltpu.VMEM((n, span), F32),
            pltpu.VMEM((n, 1, span), F32),
            pltpu.VMEM((n, 1, span), F32),
            pltpu.VMEM((groups, 1, span), F32),
            pltpu.VMEM((groups, span, 1), F32),
            pltpu.VMEM((groups, 1, span), F32),
            pltpu.VMEM((n, 1, span), F32),
            pltpu.VMEM((n, 1, span), F32),
            pltpu.VMEM((n, span), F32),
            pltpu.VMEM((owned, width), F32),
            pltpu.SemaphoreType.DMA((rows // CHUNK,)),
            pltpu.SemaphoreType.DMA,
            pltpu.SemaphoreType.DMA((groups,)),
            pltpu.SemaphoreType.DMA((2,)),
            pltpu.SemaphoreType.DMA((2,)),
        ],
        compiler_params=pltpu.CompilerParams(
            collective_id=0, has_side_effects=True, vmem_limit_bytes=60 * 1024 * 1024
        ),
    )(embeddings, cluster_ids.reshape(1, rows), cluster_slot.reshape(1, clusters))
    return best.reshape(rows), cent


def solution(mesh):
    in_specs = (P(("grp", "dev"), None), P(("grp", "dev"), None), P())
    out_specs = (P(("grp", "dev")), P(("grp", "dev"), None))
    return jax.shard_map(local, mesh=mesh, in_specs=in_specs, out_specs=out_specs, check_vma=False)
```

time: 217 us -> 118 us (0.54)
  waiting for transfers between devices: 149 us -> 0 us
  Pallas kernels: 0 us -> 114 us
  other arithmetic: 18.2 us -> 0 us
  matrix products: 14 us -> 0 us
  between operations: 14.1 us -> 0.64 us
  starting transfers between devices: 10.2 us -> 0 us
  local copies, waits for them, and re-layouts: 11.5 us -> 2.65 us
    reduce_scatter x1 -> x0, waiting for transfers between devices: 141 us -> none  [local(): lax.psum_scatter(lax.dot_general(onehot, normalized, (((0,), (0,)), ((),...]
    pallas_call x0 -> x1, Pallas kernels: none -> 114 us  [local(): pl.pallas_call(functools.partial(kernel, n_grp, n_dev, owned, quota, grou...]
    dot_general x2 -> x0, matrix products: 14 us -> none  [the longest x1 11.9 us: local(): jnp.einsum('sckd,tcld->csktl', received, received, preferred_element_type...]
    gather x1 -> x0, local copies, waits for them, and re-layouts: 10.5 us -> none  [local(): max_cosine = returned.reshape(-1)[place]]
    all_to_all x2 -> x0, starting transfers between devices: 9.99 us -> none  [the longest x1 7.43 us: local(): lax.all_to_all(outgoing.reshape(ndev, owned, MOST, width), ('grp', 'dev')...]
    scatter x1 -> x0, other arithmetic: 8.87 us -> none  [local(): jnp.zeros((clusters * MOST, width), jnp.bfloat16).at[place].set(normalized)]
    reduce_sum x5 -> x0, other arithmetic: 8.38 us -> none  [the longest x1 3.08 us: local(): live = jnp.sum(jnp.square(received.astype(jnp.float32)), axis=3) > 0.5]
    all_to_all x2 -> x0, waiting for transfers between devices: 7.48 us -> none  [the longest x1 7.48 us: local(): lax.all_to_all(jnp.transpose(maxima, (1, 0, 2)), ('grp', 'dev'), split_ax...]
  transfers between devices with their start and end apart: 3 -> 0, of which waited for: 2 -> 0; matrix products, arithmetic and copies ran while one was open for 2% -> 0% of each run, Pallas kernels for 0% -> 0%
where the time goes in v1:
time: 118 us
  Pallas kernels  114 us (97%)
  local copies, waits for them, and re-layouts  2.65 us (2%)
    pallas_call x1, Pallas kernels, local(): pl.pallas_call(functools.partial(kernel, n_grp, n_dev, owned, quota, grou...  114 us
    unnamed x2, local copies, waits for them, and re-layouts  2.65 us

profile of v1, /device:TPU:0, one launch (start us, length us, event | category | flops | bytes accessed | tf_op | source)
XLA Modules:
  0.0 117.6 jit_solution(13613517207783602465)
XLA Ops:
  0.6 114.3 %shard_map.50 = (f32[1,1024]{1,0:T(1,128)}, f32[8,1024]{1,0:T(8,128)}) custom-call(bf16[1024,1024]{1,0:T(8,128)(2,1)} %emb.1, s32[1,1024]{1,0:T(1,128)} %bitcast.3, s32[1,256]{1,0:T(1,128)} %bitcast.5), custom_call_target="tpu_custom_call" | custom-call | tf_op jit(solution)/shard_map/pallas_call | solution.py:275
  114.9 1.3 %copy.7 = f32[1024]{0:T(1024)} copy(f32[1024]{0:T(1024)} %bitcast.4) | data formatting | bytes 8192
  116.2 1.4 %copy.8 = f32[8,1024]{1,0:T(8,128)} copy(f32[8,1024]{1,0:T(8,128)} %get-tuple-element.9) | data formatting | bytes 65536

commit v2 on v1

v2 whole, which is shorter than its diff:
```python
import functools

import jax
import jax.numpy as jnp
from jax import lax
from jax.experimental import pallas as pl
from jax.experimental.pallas import tpu as pltpu
from jax.sharding import PartitionSpec as P

MOST = 8
CORES = 2
MESH = pl.DeviceIdType.MESH
F32 = jnp.float32
BF16 = jnp.bfloat16
CHUNK = 256


def iota(shape, dim):
    return lax.broadcasted_iota(jnp.int32, shape, dim)


def iotaf(shape, dim):
    return iota(shape, dim).astype(F32)


def floordiv(x, by):
    return jnp.floor((x + 0.5) * (1.0 / by))


def kernel(
    n_grp,
    n_z,
    owned,
    quota,
    part,
    group,
    emb,
    ids,
    slot_row,
    best_out,
    cent_out,
    flag_out,
    norm,
    send,
    recv,
    where_row,
    lab_mat,
    lab_send,
    lab_recv,
    lab_rows,
    lab_cols,
    best,
    ret_send,
    ret_recv,
    ret_mat,
    sums,
    load_sem,
    send_sem,
    recv_sem,
    pass_send,
    pass_recv,
    small_send,
    small_recv,
):
    chips = n_grp * n_z
    n = chips * CORES
    pair = 2 * part
    over = quota - part
    rows = norm.shape[0]
    clusters = slot_row.shape[1]
    span = group * quota
    n_groups = n // group
    group_chips = group // CORES
    my_g = lax.axis_index("grp")
    my_d = lax.axis_index("dev")
    my_z = my_d // CORES
    my_c = my_d % CORES

    def ahead(k):
        chip = k // CORES
        return (my_g + chip // n_z) % n_grp, ((my_z + chip % n_z) % n_z) * CORES + k % CORES

    def behind(k):
        chip = k // CORES
        return (
            (my_g + n_grp - chip // n_z) % n_grp,
            ((my_z + n_z - chip % n_z) % n_z) * CORES + k % CORES,
        )

    barrier = pltpu.get_barrier_semaphore()

    @pl.loop(0, n)
    def _(k):
        @pl.when(k != my_c)
        def _():
            pl.semaphore_signal(barrier, inc=1, device_id=ahead(k), device_id_type=MESH)

    def load(c):
        at = pl.ds(pl.multiple_of(c * CHUNK, CHUNK), CHUNK)
        return pltpu.make_async_copy(emb.at[at], norm.at[at], load_sem.at[c])

    @pl.loop(0, rows // CHUNK)
    def _(c):
        load(c).start()

    eye = iota((clusters, clusters), 0) == iota((clusters, clusters), 1)
    slot_col = jnp.sum(jnp.where(eye, slot_row[...].astype(F32), 0.0), axis=1, keepdims=True)

    lab_mat[...] = jnp.zeros_like(lab_mat)
    before = (iota((CHUNK, CHUNK), 0) < iota((CHUNK, CHUNK), 1)).astype(BF16)
    grp_f = my_g.astype(F32)
    z_f = my_z.astype(F32)
    core_f = my_c.astype(F32)

    def place(c, carry):
        count, filled = carry
        at = pl.ds(pl.multiple_of(c * CHUNK, CHUNK), CHUNK)
        hit = iota((clusters, CHUNK), 0) == ids[:, at]
        slot = jnp.sum(jnp.where(hit, slot_col, 0.0), axis=0, keepdims=True)
        owner = floordiv(slot, owned)
        local = slot - owner * owned
        owner_chip = floordiv(owner, CORES)
        core = owner - owner_chip * CORES
        owner_grp = floordiv(owner_chip, n_z)
        kg = owner_grp - grp_f
        kz = owner_chip - owner_grp * n_z - z_f
        kg = jnp.where(kg < 0, kg + n_grp, kg)
        kz = jnp.where(kz < 0, kz + n_z, kz)
        chip = kg * n_z + kz
        k = chip * CORES + core
        hot = (iotaf((n, CHUNK), 0) == k).astype(F32)
        earlier = jnp.dot(hot.astype(BF16), before, preferred_element_type=F32) + count
        pos = jnp.sum(hot * earlier, axis=0, keepdims=True)
        line = jnp.where(core > 0, quota - 1 - pos, pos)
        in_group = chip - floordiv(chip, group_chips) * group_chips
        lane = (in_group * CORES + core_f) * quota + line
        where_row[0:1, at] = k
        where_row[1:2, at] = lane
        where_row[2:3, at] = chip * pair + core * (pair - quota) + line
        spot = (iotaf((span, CHUNK), 0) == lane).astype(BF16)
        lab_mat[:, 0:span] += lax.dot_general(
            (hot * (local + 1.0)).astype(BF16),
            spot,
            (((1,), (1,)), ((), ())),
            preferred_element_type=F32,
        )
        count = count + jnp.sum(hot, axis=1, keepdims=True)
        to_chip = (iotaf((chips, CHUNK), 0) == chip).astype(F32)
        return count, filled + jnp.sum(to_chip, axis=1, keepdims=True)

    _, filled = lax.fori_loop(
        0, rows // CHUNK, place, (jnp.zeros((n, 1), F32), jnp.zeros((chips, 1), F32))
    )
    crowded = jnp.max((filled > pair).astype(F32), axis=0, keepdims=True)
    lab_mat[:, span:] = jnp.broadcast_to(crowded, (n, lab_mat.shape[1] - span))

    pl.semaphore_wait(barrier, n - 1)

    lab_recv[my_c] = lab_mat[pl.ds(my_c, 1), :]

    @pl.loop(0, n)
    def _(k):
        @pl.when(k != my_c)
        def _():
            lab_send[k] = lab_mat[pl.ds(k, 1), :]
            pltpu.make_async_remote_copy(
                src_ref=lab_send.at[k],
                dst_ref=lab_recv.at[(k // CORES) * CORES + my_c],
                send_sem=small_send.at[0],
                recv_sem=small_recv.at[0],
                device_id=ahead(k),
                device_id_type=MESH,
            ).start()

    @pl.loop(0, rows // CHUNK)
    def _(c):
        load(c).wait()
        at = pl.ds(pl.multiple_of(c * CHUNK, CHUNK), CHUNK)
        x = norm[at, :].astype(F32)
        norm[at, :] = (x * lax.rsqrt(jnp.sum(x * x, axis=1, keepdims=True) + 1e-06)).astype(BF16)

    made = group_chips * pair

    @pl.loop(0, n_groups)
    def _(g):
        spots = (iota((made, rows), 0) + g * made).astype(F32) == where_row[2:3, :]
        block = jnp.dot(spots.astype(BF16), norm[...], preferred_element_type=F32).astype(BF16)
        send[pl.ds(pl.multiple_of(g * made, made), made), :] = block

        @pl.when(g == 0)
        def _():
            own = send[pl.ds(pl.multiple_of(my_c * part, 16), part), :]
            recv[pl.ds(pl.multiple_of(my_c * (quota + over), 16), part), :] = own

        @pl.loop(0, group)
        def _(j):
            k = g * group + j
            core = k % CORES

            @pl.when(k != my_c)
            def _():
                to = ((k // CORES) * CORES + my_c) * quota + core * over
                pltpu.make_async_remote_copy(
                    src_ref=send.at[pl.ds(pl.multiple_of(k * part, 16), part)],
                    dst_ref=recv.at[pl.ds(pl.multiple_of(to, 16), part)],
                    send_sem=send_sem,
                    recv_sem=recv_sem.at[g],
                    device_id=ahead(k),
                    device_id_type=MESH,
                ).start()

    others = lab_recv.at[pl.ds(1, n - 1)]
    pltpu.make_async_copy(others, others, small_recv.at[0]).wait()
    diag = iota((span, span), 0) == iota((span, span), 1)
    flag_out[...] = jnp.zeros_like(flag_out)

    @pl.loop(0, n_groups)
    def _(g):
        row = lab_recv[g * group]
        for j in range(1, group):
            row = row + lab_recv[g * group + j]
        lab_rows[g] = row[:, 0:span]
        lab_cols[g] = jnp.sum(jnp.where(diag, row[:, 0:span], 0.0), axis=1, keepdims=True)
        best[g] = jnp.full((1, span), -1.0, F32)
        flag_out[...] += row[:, span:]

    sums[...] = jnp.zeros_like(sums)

    def contract(a, b):
        return lax.dot_general(a, b, (((1,), (1,)), ((), ())), preferred_element_type=F32)

    def arrive(g):
        @pl.when(g == 0)
        def _():
            got = recv.at[pl.ds(0, (group - 1) * part)]
            pltpu.make_async_copy(got, got, recv_sem.at[0]).wait()

        @pl.when(g > 0)
        def _():
            got = recv.at[pl.ds(pl.multiple_of(g * span, span), group * part)]
            pltpu.make_async_copy(got, got, recv_sem.at[g]).wait()

        if over:
            @pl.loop(0, group)
            def _(j):
                base = (g * group + j) * quota
                start = base + (pair - quota) - my_c * (pair - quota - over)
                to = base + my_c * part
                pltpu.make_async_remote_copy(
                    src_ref=recv.at[pl.ds(pl.multiple_of(start, 16), over)],
                    dst_ref=recv.at[pl.ds(pl.multiple_of(to, 16), over)],
                    send_sem=pass_send,
                    recv_sem=pass_recv.at[g],
                    device_id=(my_g, my_z * CORES + (1 - my_c)),
                    device_id_type=MESH,
                ).start()

    def compare(g):
        if over:
            got = recv.at[pl.ds(pl.multiple_of(g * span, span), group * over)]
            pltpu.make_async_copy(got, got, pass_recv.at[g]).wait()
        new = recv[pl.ds(pl.multiple_of(g * span, span), span), :]
        member = iotaf((owned, span), 0) + 1.0 == lab_rows[g]
        sums[...] += jnp.dot(member.astype(BF16), new, preferred_element_type=F32)

        keep = (lab_cols[g] == lab_rows[g]) & ~diag
        top = jnp.max(jnp.where(keep, contract(new, new), -1.0), axis=0, keepdims=True)
        best[g] = jnp.maximum(best[g], top)

        @pl.loop(0, g)
        def _(h):
            old = recv[pl.ds(pl.multiple_of(h * span, span), span), :]
            keep = lab_cols[h] == lab_rows[g]
            top = jnp.max(jnp.where(keep, contract(old, new), -1.0), axis=0, keepdims=True)
            best[g] = jnp.maximum(best[g], top)
            keep = lab_cols[g] == lab_rows[h]
            top = jnp.max(jnp.where(keep, contract(new, old), -1.0), axis=0, keepdims=True)
            best[h] = jnp.maximum(best[h], top)

    @pl.loop(0, n_groups + 1)
    def _(g):
        @pl.when(g < n_groups)
        def _():
            arrive(g)

        @pl.when(g > 0)
        def _():
            compare(g - 1)

    ret_recv[my_c] = best[0]

    @pl.loop(0, n)
    def _(k):
        @pl.when(k != my_c)
        def _():
            ret_send[k] = best[k // group]
            pltpu.make_async_remote_copy(
                src_ref=ret_send.at[k],
                dst_ref=ret_recv.at[(k // CORES) * CORES + my_c],
                send_sem=small_send.at[1],
                recv_sem=small_recv.at[1],
                device_id=behind(k),
                device_id_type=MESH,
            ).start()

    total = sums[...]
    cent_out[...] = total * lax.rsqrt(jnp.sum(total * total, axis=1, keepdims=True) + 1e-06)

    back = ret_recv.at[pl.ds(1, n - 1)]
    pltpu.make_async_copy(back, back, small_recv.at[1]).wait()

    @pl.loop(0, n)
    def _(k):
        ret_mat[pl.ds(k, 1), :] = ret_recv[k]

    @pl.loop(0, rows // CHUNK)
    def _(c):
        at = pl.ds(pl.multiple_of(c * CHUNK, CHUNK), CHUNK)
        hot = (iotaf((n, CHUNK), 0) == where_row[0:1, at]).astype(F32)
        picked = lax.dot_general(
            ret_mat[...],
            hot,
            (((0,), (0,)), ((), ())),
            precision=lax.Precision.HIGHEST,
            preferred_element_type=F32,
        )
        spot = iotaf((span, CHUNK), 0) == where_row[1:2, at]
        best_out[:, at] = jnp.sum(jnp.where(spot, picked, 0.0), axis=0, keepdims=True)

    sent = send.at[pl.ds(part, n * part - part)]
    pltpu.make_async_copy(sent, sent, send_sem).wait()
    if over:
        sent = recv.at[pl.ds(0, n * over)]
        pltpu.make_async_copy(sent, sent, pass_send).wait()
    sent = lab_send.at[pl.ds(1, n - 1)]
    pltpu.make_async_copy(sent, sent, small_send.at[0]).wait()
    sent = ret_send.at[pl.ds(1, n - 1)]
    pltpu.make_async_copy(sent, sent, small_send.at[1]).wait()


def exchange(embeddings, ids, slot_row, part, number):
    n_grp = lax.axis_size("grp")
    n_z = lax.axis_size("dev") // CORES
    n = n_grp * n_z * CORES
    rows, width = embeddings.shape
    clusters = slot_row.shape[1]
    owned = clusters // n
    quota = owned * MOST
    group = 4
    span = group * quota
    groups = n // group
    vmem = pl.BlockSpec(memory_space=pltpu.VMEM)
    return pl.pallas_call(
        functools.partial(kernel, n_grp, n_z, owned, quota, part, group),
        out_shape=(
            jax.ShapeDtypeStruct((1, rows), F32),
            jax.ShapeDtypeStruct((owned, width), F32),
            jax.ShapeDtypeStruct((1, 128), F32),
        ),
        in_specs=[pl.BlockSpec(memory_space=pl.ANY), vmem, vmem],
        out_specs=(vmem, vmem, vmem),
        scratch_shapes=[
            pltpu.VMEM((rows, width), BF16),
            pltpu.VMEM((n * part, width), BF16),
            pltpu.VMEM((n * quota, width), BF16),
            pltpu.VMEM((8, rows), F32),
            pltpu.VMEM((n, span + 128), F32),
            pltpu.VMEM((n, 1, span + 128), F32),
            pltpu.VMEM((n, 1, span + 128), F32),
            pltpu.VMEM((groups, 1, span), F32),
            pltpu.VMEM((groups, span, 1), F32),
            pltpu.VMEM((groups, 1, span), F32),
            pltpu.VMEM((n, 1, span), F32),
            pltpu.VMEM((n, 1, span), F32),
            pltpu.VMEM((n, span), F32),
            pltpu.VMEM((owned, width), F32),
            pltpu.SemaphoreType.DMA((rows // CHUNK,)),
            pltpu.SemaphoreType.DMA,
            pltpu.SemaphoreType.DMA((groups,)),
            pltpu.SemaphoreType.DMA,
            pltpu.SemaphoreType.DMA((groups,)),
            pltpu.SemaphoreType.DMA((2,)),
            pltpu.SemaphoreType.DMA((2,)),
        ],
        compiler_params=pltpu.CompilerParams(
            collective_id=number, has_side_effects=True, vmem_limit_bytes=60 * 1024 * 1024
        ),
    )(embeddings, ids, slot_row)


def local(embeddings, cluster_ids, cluster_slot):
    rows = embeddings.shape[0]
    clusters = cluster_slot.shape[0]
    ids = cluster_ids.reshape(1, rows)
    slot_row = cluster_slot.reshape(1, clusters)
    quota = clusters // lax.axis_size(("grp", "dev")) * MOST
    best, cent, crowded = exchange(embeddings, ids, slot_row, quota * 3 // 4, 0)

    def whole():
        again = exchange(embeddings, ids, slot_row, quota, 1)
        return again[0], again[1]

    best, cent = lax.cond(crowded[0, 0] > 0, whole, lambda: (best, cent))
    return best.reshape(rows), cent


def solution(mesh):
    in_specs = (P(("grp", "dev"), None), P(("grp", "dev"), None), P())
    out_specs = (P(("grp", "dev")), P(("grp", "dev"), None))
    return jax.shard_map(local, mesh=mesh, in_specs=in_specs, out_specs=out_specs, check_vma=False)
```

time: 118 us -> 97.6 us (0.83)
  Pallas kernels: 114 us -> 95 us
  local copies, waits for them, and re-layouts: 2.65 us -> 1.22 us
    pallas_call x1, Pallas kernels: 114 us -> 95 us  [exchange(): pl.pallas_call(functools.partial(kernel, n_grp, n_z, owned, quota, part,...]
    unnamed x2 -> x8, local copies, waits for them, and re-layouts: 2.65 us -> 1.22 us
where the time goes in v2:
time: 97.6 us; the launch traced here: 97.4 us
  Pallas kernels  95 us (97%)
  between operations  1.25 us (1%)
  local copies, waits for them, and re-layouts  1.22 us (1%)
    pallas_call x1, Pallas kernels, exchange(): pl.pallas_call(functools.partial(kernel, n_grp, n_z, owned, quota, part,...  95 us

profile of v2, /device:TPU:0, one launch (start us, length us, event | category | flops | bytes accessed | tf_op | source)
XLA Modules:
  0.0 97.4 jit_solution(13555307108930818990)
XLA Ops:
  0.6 0.0 copy-start
  0.6 0.0 copy-start.2
  0.6 0.0 copy-start.1
  0.7 95.0 %shard_map.50 = (f32[1,1024]{1,0:T(1,128)S(1)}, f32[8,1024]{1,0:T(8,128)S(1)}, f32[1,128]{1,0:T(1,128)}) custom-call(bf16[1024,1024]{1,0:T(8,128)(2,1)} %emb.1, s32[1,1024]{1,0:T(1,128)} %bitcast.5, s32[1,256]{1,0:T(1,128)} %bitcast.7), custom_call_target="tpu_custom_call" | custom-call | tf_op jit(solution)/shard_map/pallas_call | solution.py:353
  96.2 0.0 copy-done
  96.2 0.0 copy-done.2
  96.2 0.0 copy-done.1
  96.2 0.6 copy.11
  96.8 0.6 copy.12
  (1 shorter events, 0.0 us)
Async XLA Ops:
  0.6 95.6 %copy-start = (bf16[1024,1024]{1,0:T(8,128)(2,1)S(1)}, bf16[1024,1024]{1,0:T(8,128)(2,1)}, u32[]{:S(2)}) copy-start(bf16[1024,1024]{1,0:T(8,128)(2,1)} %emb.1) | copy-start | bytes 6291460
  0.6 95.6 %copy-start.2 = (s32[256]{0:T(256)S(1)}, s32[256]{0:T(256)}, u32[]{:S(2)}) copy-start(s32[256]{0:T(256)} %param.7) | copy-start | bytes 3076
  0.6 95.6 %copy-start.1 = (s32[1024,1]{0,1:T(1,128)S(1)}, s32[1024,1]{0,1:T(1,128)}, u32[]{:S(2)}) copy-start(s32[1024,1]{0,1:T(1,128)} %param.6) | copy-start | bytes 12292

commit v3 on v2

--- a/solution.py
+++ b/solution.py
@@ -50,7 +50,6 @@
     lab_rows,
     lab_cols,
     best,
-    ret_send,
     ret_recv,
     ret_mat,
     sums,
@@ -73,23 +72,22 @@
     group_chips = group // CORES
     my_g = lax.axis_index("grp")
     my_d = lax.axis_index("dev")
-    my_z = my_d // CORES
-    my_c = my_d % CORES
+    my_z = lax.div(my_d, CORES)
+    my_c = lax.rem(my_d, CORES)
 
     def ahead(k):
-        chip = k // CORES
-        return (my_g + chip // n_z) % n_grp, ((my_z + chip % n_z) % n_z) * CORES + k % CORES
+        chip, core = lax.div(k, CORES), lax.rem(k, CORES)
+        to_g = lax.rem(my_g + lax.div(chip, n_z), n_grp)
+        return to_g, lax.rem(my_z + chip, n_z) * CORES + core
 
     def behind(k):
-        chip = k // CORES
-        return (
-            (my_g + n_grp - chip // n_z) % n_grp,
-            ((my_z + n_z - chip % n_z) % n_z) * CORES + k % CORES,
-        )
+        chip, core = lax.div(k, CORES), lax.rem(k, CORES)
+        to_g = lax.rem(my_g + n_grp - lax.div(chip, n_z), n_grp)
+        return to_g, lax.rem(my_z + n_z - lax.rem(chip, n_z), n_z) * CORES + core
 
     barrier = pltpu.get_barrier_semaphore()
 
-    @pl.loop(0, n)
+    @pl.loop(0, n, unroll=8)
     def _(k):
         @pl.when(k != my_c)
         def _():
@@ -154,24 +152,6 @@
     crowded = jnp.max((filled > pair).astype(F32), axis=0, keepdims=True)
     lab_mat[:, span:] = jnp.broadcast_to(crowded, (n, lab_mat.shape[1] - span))
 
-    pl.semaphore_wait(barrier, n - 1)
-
-    lab_recv[my_c] = lab_mat[pl.ds(my_c, 1), :]
-
-    @pl.loop(0, n)
-    def _(k):
-        @pl.when(k != my_c)
-        def _():
-            lab_send[k] = lab_mat[pl.ds(k, 1), :]
-            pltpu.make_async_remote_copy(
-                src_ref=lab_send.at[k],
-                dst_ref=lab_recv.at[(k // CORES) * CORES + my_c],
-                send_sem=small_send.at[0],
-                recv_sem=small_recv.at[0],
-                device_id=ahead(k),
-                device_id_type=MESH,
-            ).start()
-
     @pl.loop(0, rows // CHUNK)
     def _(c):
         load(c).wait()
@@ -181,25 +161,20 @@
 
     made = group_chips * pair
 
-    @pl.loop(0, n_groups)
-    def _(g):
+    def make(g):
         spots = (iota((made, rows), 0) + g * made).astype(F32) == where_row[2:3, :]
         block = jnp.dot(spots.astype(BF16), norm[...], preferred_element_type=F32).astype(BF16)
         send[pl.ds(pl.multiple_of(g * made, made), made), :] = block
 
-        @pl.when(g == 0)
-        def _():
-            own = send[pl.ds(pl.multiple_of(my_c * part, 16), part), :]
-            recv[pl.ds(pl.multiple_of(my_c * (quota + over), 16), part), :] = own
-
-        @pl.loop(0, group)
+    def ship(g):
+        @pl.loop(0, group, unroll=True)
         def _(j):
             k = g * group + j
-            core = k % CORES
+            twin = lax.div(k, CORES) * CORES + my_c
 
             @pl.when(k != my_c)
             def _():
-                to = ((k // CORES) * CORES + my_c) * quota + core * over
+                to = twin * quota + lax.rem(k, CORES) * over
                 pltpu.make_async_remote_copy(
                     src_ref=send.at[pl.ds(pl.multiple_of(k * part, 16), part)],
                     dst_ref=recv.at[pl.ds(pl.multiple_of(to, 16), part)],
@@ -208,6 +183,38 @@
                     device_id=ahead(k),
                     device_id_type=MESH,
                 ).start()
+
+    make(0)
+    own = send[pl.ds(pl.multiple_of(my_c * part, 16), part), :]
+    recv[pl.ds(pl.multiple_of(my_c * (quota + over), 16), part), :] = own
+    lab_recv[my_c] = lab_mat[pl.ds(my_c, 1), :]
+
+    @pl.loop(0, n, unroll=8)
+    def _(k):
+        lab_send[k] = lab_mat[pl.ds(k, 1), :]
+
+    pl.semaphore_wait(barrier, n - 1)
+    ship(0)
+
+    @pl.loop(1, n_groups)
+    def _(g):
+        make(g)
+        ship(g)
+
+        @pl.when(g == 1)
+        def _():
+            @pl.loop(0, n, unroll=8)
+            def _(k):
+                @pl.when(k != my_c)
+                def _():
+                    pltpu.make_async_remote_copy(
+                        src_ref=lab_send.at[k],
+                        dst_ref=lab_recv.at[lax.div(k, CORES) * CORES + my_c],
+                        send_sem=small_send.at[0],
+                        recv_sem=small_recv.at[0],
+                        device_id=ahead(k),
+                        device_id_type=MESH,
+                    ).start()
 
     others = lab_recv.at[pl.ds(1, n - 1)]
     pltpu.make_async_copy(others, others, small_recv.at[0]).wait()
@@ -241,7 +248,7 @@
             pltpu.make_async_copy(got, got, recv_sem.at[g]).wait()
 
         if over:
-            @pl.loop(0, group)
+            @pl.loop(0, group, unroll=True)
             def _(j):
                 base = (g * group + j) * quota
                 start = base + (pair - quota) - my_c * (pair - quota - over)
@@ -277,26 +284,20 @@
             top = jnp.max(jnp.where(keep, contract(new, old), -1.0), axis=0, keepdims=True)
             best[h] = jnp.maximum(best[h], top)
 
-    @pl.loop(0, n_groups + 1)
+    @pl.loop(0, n_groups)
     def _(g):
-        @pl.when(g < n_groups)
-        def _():
-            arrive(g)
-
-        @pl.when(g > 0)
-        def _():
-            compare(g - 1)
+        arrive(g)
+        compare(g)
 
     ret_recv[my_c] = best[0]
 
-    @pl.loop(0, n)
+    @pl.loop(0, n, unroll=8)
     def _(k):
         @pl.when(k != my_c)
         def _():
-            ret_send[k] = best[k // group]
             pltpu.make_async_remote_copy(
-                src_ref=ret_send.at[k],
-                dst_ref=ret_recv.at[(k // CORES) * CORES + my_c],
+                src_ref=best.at[lax.div(k, group)],
+                dst_ref=ret_recv.at[lax.div(k, CORES) * CORES + my_c],
                 send_sem=small_send.at[1],
                 recv_sem=small_recv.at[1],
                 device_id=behind(k),
@@ -309,7 +310,7 @@
     back = ret_recv.at[pl.ds(1, n - 1)]
     pltpu.make_async_copy(back, back, small_recv.at[1]).wait()
 
-    @pl.loop(0, n)
+    @pl.loop(0, n, unroll=8)
     def _(k):
         ret_mat[pl.ds(k, 1), :] = ret_recv[k]
 
@@ -334,7 +335,7 @@
         pltpu.make_async_copy(sent, sent, pass_send).wait()
     sent = lab_send.at[pl.ds(1, n - 1)]
     pltpu.make_async_copy(sent, sent, small_send.at[0]).wait()
-    sent = ret_send.at[pl.ds(1, n - 1)]
+    sent = ret_recv.at[pl.ds(1, n - 1)]
     pltpu.make_async_copy(sent, sent, small_send.at[1]).wait()
 
 
@@ -371,7 +372,6 @@
             pltpu.VMEM((groups, span, 1), F32),
             pltpu.VMEM((groups, 1, span), F32),
             pltpu.VMEM((n, 1, span), F32),
-            pltpu.VMEM((n, 1, span), F32),
             pltpu.VMEM((n, span), F32),
             pltpu.VMEM((owned, width), F32),
             pltpu.SemaphoreType.DMA((rows // CHUNK,)),

time: 97.6 us -> 94.8 us (0.971)
  Pallas kernels: 95 us -> 92.2 us
    pallas_call x1, Pallas kernels: 95 us -> 92.2 us  [exchange(): pl.pallas_call(functools.partial(kernel, n_grp, n_z, owned, quota, part,...]
where the time goes in v3:
time: 94.8 us; the launch traced here: 94.7 us
  Pallas kernels  92.2 us (97%)
  between operations  1.25 us (1%)
  local copies, waits for them, and re-layouts  1.22 us (1%)
    pallas_call x1, Pallas kernels, exchange(): pl.pallas_call(functools.partial(kernel, n_grp, n_z, owned, quota, part,...  92.2 us

profile of v3, /device:TPU:0, one launch (start us, length us, event | category | flops | bytes accessed | tf_op | source)
XLA Modules:
  0.0 94.7 jit_solution(5045994017254104978)
XLA Ops:
  0.6 0.0 copy-start
  0.6 0.0 copy-start.2
  0.6 0.0 copy-start.1
  0.7 92.2 %shard_map.50 = (f32[1,1024]{1,0:T(1,128)S(1)}, f32[8,1024]{1,0:T(8,128)S(1)}, f32[1,128]{1,0:T(1,128)}) custom-call(bf16[1024,1024]{1,0:T(8,128)(2,1)} %emb.1, s32[1,1024]{1,0:T(1,128)} %bitcast.5, s32[1,256]{1,0:T(1,128)} %bitcast.7), custom_call_target="tpu_custom_call" | custom-call | tf_op jit(solution)/shard_map/pallas_call | solution.py:354
  93.4 0.0 copy-done
  93.4 0.0 copy-done.2
  93.4 0.0 copy-done.1
  93.5 0.6 copy.11
  94.1 0.6 copy.12
  (1 shorter events, 0.0 us)
Async XLA Ops:
  0.6 92.8 %copy-start = (bf16[1024,1024]{1,0:T(8,128)(2,1)S(1)}, bf16[1024,1024]{1,0:T(8,128)(2,1)}, u32[]{:S(2)}) copy-start(bf16[1024,1024]{1,0:T(8,128)(2,1)} %emb.1) | copy-start | bytes 6291460
  0.6 92.8 %copy-start.2 = (s32[256]{0:T(256)S(1)}, s32[256]{0:T(256)}, u32[]{:S(2)}) copy-start(s32[256]{0:T(256)} %param.7) | copy-start | bytes 3076
  0.6 92.8 %copy-start.1 = (s32[1024,1]{0,1:T(1,128)S(1)}, s32[1024,1]{0,1:T(1,128)}, u32[]{:S(2)}) copy-start(s32[1024,1]{0,1:T(1,128)} %param.6) | copy-start | bytes 12292

commit v4 on v3

--- a/solution.py
+++ b/solution.py
@@ -262,6 +262,22 @@
                     device_id_type=MESH,
                 ).start()
 
+    def give(g):
+        @pl.loop(0, group, unroll=True)
+        def _(j):
+            k = g * group + j
+
+            @pl.when(k != my_c)
+            def _():
+                pltpu.make_async_remote_copy(
+                    src_ref=best.at[g],
+                    dst_ref=ret_recv.at[lax.div(k, CORES) * CORES + my_c],
+                    send_sem=small_send.at[1],
+                    recv_sem=small_recv.at[1],
+                    device_id=behind(k),
+                    device_id_type=MESH,
+                ).start()
+
     def compare(g):
         if over:
             got = recv.at[pl.ds(pl.multiple_of(g * span, span), group * over)]
@@ -284,25 +300,20 @@
             top = jnp.max(jnp.where(keep, contract(new, old), -1.0), axis=0, keepdims=True)
             best[h] = jnp.maximum(best[h], top)
 
+            @pl.when(g == n_groups - 1)
+            def _():
+                give(h)
+
+        @pl.when(g == n_groups - 1)
+        def _():
+            give(g)
+
     @pl.loop(0, n_groups)
     def _(g):
         arrive(g)
         compare(g)
 
     ret_recv[my_c] = best[0]
-
-    @pl.loop(0, n, unroll=8)
-    def _(k):
-        @pl.when(k != my_c)
-        def _():
-            pltpu.make_async_remote_copy(
-                src_ref=best.at[lax.div(k, group)],
-                dst_ref=ret_recv.at[lax.div(k, CORES) * CORES + my_c],
-                send_sem=small_send.at[1],
-                recv_sem=small_recv.at[1],
-                device_id=behind(k),
-                device_id_type=MESH,
-            ).start()
 
     total = sums[...]
     cent_out[...] = total * lax.rsqrt(jnp.sum(total * total, axis=1, keepdims=True) + 1e-06)

time: 94.8 us -> 94.9 us (level)
  no operation moved by 1% of the time
where the time goes in v4:
time: 94.9 us; the launch traced here: 94.7 us
  Pallas kernels  92.2 us (97%)
  between operations  1.25 us (1%)
  local copies, waits for them, and re-layouts  1.22 us (1%)
    pallas_call x1, Pallas kernels, exchange(): pl.pallas_call(functools.partial(kernel, n_grp, n_z, owned, quota, part,...  92.2 us

profile of v4, /device:TPU:0, one launch (start us, length us, event | category | flops | bytes accessed | tf_op | source)
XLA Modules:
  0.0 94.7 jit_solution(4207917442391586027)
XLA Ops:
  0.6 0.0 copy-start
  0.6 0.0 copy-start.2
  0.6 0.0 copy-start.1
  0.7 92.2 %shard_map.50 = (f32[1,1024]{1,0:T(1,128)S(1)}, f32[8,1024]{1,0:T(8,128)S(1)}, f32[1,128]{1,0:T(1,128)}) custom-call(bf16[1024,1024]{1,0:T(8,128)(2,1)} %emb.1, s32[1,1024]{1,0:T(1,128)} %bitcast.5, s32[1,256]{1,0:T(1,128)} %bitcast.7), custom_call_target="tpu_custom_call" | custom-call | tf_op jit(solution)/shard_map/pallas_call | solution.py:365
  93.4 0.0 copy-done
  93.4 0.0 copy-done.2
  93.5 0.0 copy-done.1
  93.5 0.6 copy.11
  94.1 0.6 copy.12
  (1 shorter events, 0.0 us)
Async XLA Ops:
  0.6 92.8 %copy-start = (bf16[1024,1024]{1,0:T(8,128)(2,1)S(1)}, bf16[1024,1024]{1,0:T(8,128)(2,1)}, u32[]{:S(2)}) copy-start(bf16[1024,1024]{1,0:T(8,128)(2,1)} %emb.1) | copy-start | bytes 6291460
  0.6 92.8 %copy-start.2 = (s32[256]{0:T(256)S(1)}, s32[256]{0:T(256)}, u32[]{:S(2)}) copy-start(s32[256]{0:T(256)} %param.7) | copy-start | bytes 3076
  0.6 92.8 %copy-start.1 = (s32[1024,1]{0,1:T(1,128)S(1)}, s32[1024,1]{0,1:T(1,128)}, u32[]{:S(2)}) copy-start(s32[1024,1]{0,1:T(1,128)} %param.6) | copy-start | bytes 12292

commit v5 on v4

--- a/solution.py
+++ b/solution.py
@@ -194,27 +194,25 @@
         lab_send[k] = lab_mat[pl.ds(k, 1), :]
 
     pl.semaphore_wait(barrier, n - 1)
+    @pl.loop(0, n, unroll=8)
+    def _(k):
+        @pl.when(k != my_c)
+        def _():
+            pltpu.make_async_remote_copy(
+                src_ref=lab_send.at[k],
+                dst_ref=lab_recv.at[lax.div(k, CORES) * CORES + my_c],
+                send_sem=small_send.at[0],
+                recv_sem=small_recv.at[0],
+                device_id=ahead(k),
+                device_id_type=MESH,
+            ).start()
+
     ship(0)
 
     @pl.loop(1, n_groups)
     def _(g):
         make(g)
         ship(g)
-
-        @pl.when(g == 1)
-        def _():
-            @pl.loop(0, n, unroll=8)
-            def _(k):
-                @pl.when(k != my_c)
-                def _():
-                    pltpu.make_async_remote_copy(
-                        src_ref=lab_send.at[k],
-                        dst_ref=lab_recv.at[lax.div(k, CORES) * CORES + my_c],
-                        send_sem=small_send.at[0],
-                        recv_sem=small_recv.at[0],
-                        device_id=ahead(k),
-                        device_id_type=MESH,
-                    ).start()
 
     others = lab_recv.at[pl.ds(1, n - 1)]
     pltpu.make_async_copy(others, others, small_recv.at[0]).wait()

time: 94.9 us -> 94.6 us (level)
  no operation moved by 1% of the time
where the time goes in v5:
time: 94.6 us; the launch traced here: 94.4 us
  Pallas kernels  91.9 us (97%)
  between operations  1.25 us (1%)
  local copies, waits for them, and re-layouts  1.22 us (1%)
    pallas_call x1, Pallas kernels, exchange(): pl.pallas_call(functools.partial(kernel, n_grp, n_z, owned, quota, part,...  91.9 us

profile of v5, /device:TPU:0, one launch (start us, length us, event | category | flops | bytes accessed | tf_op | source)
XLA Modules:
  0.0 94.4 jit_solution(17449443300780603885)
XLA Ops:
  0.6 0.0 copy-start
  0.6 0.0 copy-start.2
  0.6 0.0 copy-start.1
  0.7 91.9 %shard_map.50 = (f32[1,1024]{1,0:T(1,128)S(1)}, f32[8,1024]{1,0:T(8,128)S(1)}, f32[1,128]{1,0:T(1,128)}) custom-call(bf16[1024,1024]{1,0:T(8,128)(2,1)} %emb.1, s32[1,1024]{1,0:T(1,128)} %bitcast.5, s32[1,256]{1,0:T(1,128)} %bitcast.7), custom_call_target="tpu_custom_call" | custom-call | tf_op jit(solution)/shard_map/pallas_call | solution.py:363
  93.2 0.0 copy-done
  93.2 0.0 copy-done.2
  93.2 0.0 copy-done.1
  93.2 0.6 copy.11
  93.8 0.6 copy.12
  (1 shorter events, 0.0 us)
Async XLA Ops:
  0.6 92.5 %copy-start = (bf16[1024,1024]{1,0:T(8,128)(2,1)S(1)}, bf16[1024,1024]{1,0:T(8,128)(2,1)}, u32[]{:S(2)}) copy-start(bf16[1024,1024]{1,0:T(8,128)(2,1)} %emb.1) | copy-start | bytes 6291460
  0.6 92.5 %copy-start.2 = (s32[256]{0:T(256)S(1)}, s32[256]{0:T(256)}, u32[]{:S(2)}) copy-start(s32[256]{0:T(256)} %param.7) | copy-start | bytes 3076
  0.6 92.5 %copy-start.1 = (s32[1024,1]{0,1:T(1,128)S(1)}, s32[1024,1]{0,1:T(1,128)}, u32[]{:S(2)}) copy-start(s32[1024,1]{0,1:T(1,128)} %param.6) | copy-start | bytes 12292

commit v6 on v5

--- a/solution.py
+++ b/solution.py
@@ -77,12 +77,13 @@
 
     def ahead(k):
         chip, core = lax.div(k, CORES), lax.rem(k, CORES)
-        to_g = lax.rem(my_g + lax.div(chip, n_z), n_grp)
+        to_g = lax.rem(my_g + lax.div(chip, n_z) + lax.rem(chip, n_z), n_grp)
         return to_g, lax.rem(my_z + chip, n_z) * CORES + core
 
     def behind(k):
         chip, core = lax.div(k, CORES), lax.rem(k, CORES)
-        to_g = lax.rem(my_g + n_grp - lax.div(chip, n_z), n_grp)
+        back = lax.rem(lax.div(chip, n_z) + lax.rem(chip, n_z), n_grp)
+        to_g = lax.rem(my_g + n_grp - back, n_grp)
         return to_g, lax.rem(my_z + n_z - lax.rem(chip, n_z), n_z) * CORES + core
 
     barrier = pltpu.get_barrier_semaphore()
@@ -124,7 +125,8 @@
         kz = owner_chip - owner_grp * n_z - z_f
         kg = jnp.where(kg < 0, kg + n_grp, kg)
         kz = jnp.where(kz < 0, kz + n_z, kz)
-        chip = kg * n_z + kz
+        turn = kg + n_z * n_grp - kz
+        chip = (turn - floordiv(turn, n_grp) * n_grp) * n_z + kz
         k = chip * CORES + core
         hot = (iotaf((n, CHUNK), 0) == k).astype(F32)
         earlier = jnp.dot(hot.astype(BF16), before, preferred_element_type=F32) + count

time: 94.6 us -> 95.1 us (level)
  no operation moved by 1% of the time
where the time goes in v6:
time: 95.1 us; the launch traced here: 95 us
  Pallas kernels  92.5 us (97%)
  between operations  1.25 us (1%)
  local copies, waits for them, and re-layouts  1.22 us (1%)
    pallas_call x1, Pallas kernels, exchange(): pl.pallas_call(functools.partial(kernel, n_grp, n_z, owned, quota, part,...  92.5 us

profile of v6, /device:TPU:0, one launch (start us, length us, event | category | flops | bytes accessed | tf_op | source)
XLA Modules:
  0.0 95.0 jit_solution(3043582039814719414)
XLA Ops:
  0.6 0.0 copy-start
  0.6 0.0 copy-start.2
  0.6 0.0 copy-start.1
  0.7 92.5 %shard_map.50 = (f32[1,1024]{1,0:T(1,128)S(1)}, f32[8,1024]{1,0:T(8,128)S(1)}, f32[1,128]{1,0:T(1,128)}) custom-call(bf16[1024,1024]{1,0:T(8,128)(2,1)} %emb.1, s32[1,1024]{1,0:T(1,128)} %bitcast.5, s32[1,256]{1,0:T(1,128)} %bitcast.7), custom_call_target="tpu_custom_call" | custom-call | tf_op jit(solution)/shard_map/pallas_call | solution.py:365
  93.7 0.0 copy-done
  93.7 0.0 copy-done.2
  93.7 0.0 copy-done.1
  93.7 0.6 copy.11
  94.3 0.6 copy.12
  (1 shorter events, 0.0 us)
Async XLA Ops:
  0.6 93.1 %copy-start = (bf16[1024,1024]{1,0:T(8,128)(2,1)S(1)}, bf16[1024,1024]{1,0:T(8,128)(2,1)}, u32[]{:S(2)}) copy-start(bf16[1024,1024]{1,0:T(8,128)(2,1)} %emb.1) | copy-start | bytes 6291460
  0.6 93.1 %copy-start.2 = (s32[256]{0:T(256)S(1)}, s32[256]{0:T(256)}, u32[]{:S(2)}) copy-start(s32[256]{0:T(256)} %param.7) | copy-start | bytes 3076
  0.6 93.1 %copy-start.1 = (s32[1024,1]{0,1:T(1,128)S(1)}, s32[1024,1]{0,1:T(1,128)}, u32[]{:S(2)}) copy-start(s32[1024,1]{0,1:T(1,128)} %param.6) | copy-start | bytes 12292
